TPU v7x, 512 devices: a whole 4x8x8 slice. The times are simulated.
512 devices in a mesh: dp: 4 (over x), row: 16 (over y, core), col: 8 (over z).
Axes of the slice: x: 4, y: 8, z: 8, core: 2. Of those that a mesh axis runs over, the one named last changes fastest.
Arguments:
- grad_wi: bfloat16 [4, 4096, 16384], P('dp', 'row', 'col'), may hold values from -100 to 100
- grad_wo: bfloat16 [4, 16384, 4096], P('dp', 'row', 'col'), may hold values from -100 to 100
- row_wi: float32 [4096], P('row'), may hold values from 0.01 to 1
- col_wi: float32 [16384], P('col'), may hold values from 0.01 to 1
- row_wo: float32 [16384], P('row'), may hold values from 0.01 to 1
- col_wo: float32 [4096], P('col'), may hold values from 0.01 to 1
Outputs:
- update_wi: bfloat16 [4096, 16384], P('row', 'col')
- row_wi_new: float32 [4096], P('row')
- col_wi_new: float32 [16384], P('col')
- update_wo: bfloat16 [16384, 4096], P('row', 'col')
- row_wo_new: float32 [16384], P('row')
- col_wo_new: float32 [4096], P('col')
All inputs are finite; a program needn't handle non-finite values.
Results may differ from a plain program's by a relative error of at most 0.015.
Values may be sent and summed in bfloat16 or wider, within the bound.
A program may use at most 64 MiB of HBM per device.

v0:
```python
import jax
import jax.numpy as jnp
from jax import lax
from jax.sharding import PartitionSpec as P

D = 4096
FF = 16384


BETA = 0.8
EPS_SQUARE = 1e-30


def column_totals(square_wi, square_wo):
    return lax.psum((jnp.sum(square_wi, axis=0), jnp.sum(square_wo, axis=0)), "row")


def local(grad_wi, grad_wo, row_wi, col_wi, row_wo, col_wo):
    terms = (grad_wi[0].astype(jnp.float32), grad_wo[0].astype(jnp.float32))
    total_wi, total_wo = (
        lax.psum(terms[0].astype(jnp.bfloat16), "dp").astype(jnp.float32),
        lax.psum(terms[1].astype(jnp.bfloat16), "dp").astype(jnp.float32),
    )
    square_wi = total_wi * total_wi + EPS_SQUARE
    square_wo = total_wo * total_wo + EPS_SQUARE
    row_sum_wi, row_sum_wo = lax.psum(
        (jnp.sum(square_wi, axis=1), jnp.sum(square_wo, axis=1)), "col"
    )
    col_sum_wi, col_sum_wo = column_totals(square_wi, square_wo)
    row_new_wi = BETA * row_wi + (1.0 - BETA) * (row_sum_wi / FF)
    row_new_wo = BETA * row_wo + (1.0 - BETA) * (row_sum_wo / D)
    col_new_wi = BETA * col_wi + (1.0 - BETA) * (col_sum_wi / D)
    col_new_wo = BETA * col_wo + (1.0 - BETA) * (col_sum_wo / FF)
    raw_wi = total_wi / jnp.sqrt(row_new_wi[:, None] * col_new_wi[None, :])
    raw_wo = total_wo / jnp.sqrt(row_new_wo[:, None] * col_new_wo[None, :])
    local_squares = (jnp.sum(raw_wi * raw_wi), jnp.sum(raw_wo * raw_wo))
    energy_wi, energy_wo = lax.psum((local_squares[0], local_squares[1]), ("row", "col"))
    update_wi = (raw_wi / jnp.maximum(1.0, jnp.sqrt(energy_wi / (D * FF)))).astype(jnp.bfloat16)
    update_wo = (raw_wo / jnp.maximum(1.0, jnp.sqrt(energy_wo / (D * FF)))).astype(jnp.bfloat16)
    return (update_wi, row_new_wi, col_new_wi, update_wo, row_new_wo, col_new_wo)


def solution(mesh):
    return jax.shard_map(
        local,
        mesh=mesh,
        in_specs=(
            P("dp", "row", "col"),
            P("dp", "row", "col"),
            P("row"),
            P("col"),
            P("row"),
            P("col"),
        ),
        out_specs=(P("row", "col"), P("row"), P("col"), P("row", "col"), P("row"), P("col")),
        check_vma=False,
    )
```

profile of v0, /device:TPU:1, one launch (start us, length us, event | category | flops | bytes accessed | tf_op | source)
XLA Modules:
  0.0 405.3 jit_solution(8415651941492895730)
XLA Ops:
  7.2 0.0 all-reduce.6.cloned.1.call-start
  7.2 0.7 all-reduce.6.cloned.1.call-update
  7.9 77.6 %all-reduce.6.cloned.1.call-done = (bf16[256,2048]{1,0:T(8,128)(2,1)}, bf16[1024,512]{1,0:T(8,128)(2,1)}) async-done(((bf16[256,2048]{1,0:T(8,128)(2,1)}, bf16[1024,512]{1,0:T(8,128)(2,1)}), (bf16[256,2048]{1,0:T(8,128)(2,1)}, bf16[1024,512]{1,0:T(8,128)(2,1)})) %all-reduce.6.cloned.1.call-update) | async-done | bytes 2097168 | tf_op jit(solution)/shard_map/psum | solution.py:21
  85.5 0.0 copy-start.1
  85.5 0.0 copy-start.9
  85.5 0.0 copy-start.7
  85.5 0.0 copy-start.6
  85.5 1.8 fusion.5
  87.3 0.0 copy-done.1
  87.3 0.0 copy-start.8
  87.3 0.0 copy-start
  87.4 0.5 fusion.2
  87.9 14.6 %all-reduce.2 = (f32[256]{0:T(256)S(1)}, f32[1024]{0:T(1024)S(1)}) all-reduce(f32[256]{0:T(256)S(1)} %get-tuple-element.8, f32[1024]{0:T(1024)S(1)} %get-tuple-element.6), channel_id=1, replica_groups=mesh['dp'=4,'row'=16,'col'=8] {'col'}, use_global_device_ids=true, to_apply=%region_2.0 | all-reduce | flops 1280 | bytes 10240 | tf_op jit(solution)/shard_map/psum | solution.py:26
  102.5 0.0 copy-done.9
  102.5 0.0 copy-start.5
  102.5 0.0 copy-done.7
  102.5 0.0 copy-start.3
  102.5 46.7 %all-reduce.1 = (f32[2048]{0:T(1024)S(1)}, f32[512]{0:T(512)S(1)}) all-reduce(f32[2048]{0:T(1024)S(1)} %get-tuple-element.9, f32[512]{0:T(512)S(1)} %get-tuple-element.7), channel_id=1, replica_groups=mesh['dp'=4,'row'=16,'col'=8] {'row'}, use_global_device_ids=true, to_apply=%region_4.0 | all-reduce | flops 2560 | bytes 20480 | tf_op jit(solution)/shard_map/psum | solution.py:15
  149.2 0.0 copy-done.6
  149.2 0.0 copy-start.2
  149.2 1.5 multiply_reduce_fusion.1
  150.7 0.0 copy-done.8
  150.7 0.0 copy-done
  150.7 0.0 copy-start.4
  150.8 1.4 multiply_reduce_fusion
  152.2 242.0 %all-reduce = (f32[]{:T(128)}, f32[]{:T(128)}) all-reduce(f32[]{:T(128)} %multiply_reduce_fusion.1, f32[]{:T(128)} %multiply_reduce_fusion), channel_id=1, replica_groups=mesh['dp'=4,'row'=16,'col'=8] {'row','col'}, use_global_device_ids=true, to_apply=%region_6.0 | all-reduce | flops 2 | bytes 16 | tf_op jit(solution)/shard_map/psum | solution.py:37
  395.6 0.0 copy-done.5
  395.6 0.0 copy-done.2
  395.6 1.4 divide_convert_fusion.1
  397.0 0.0 copy-done.3
  397.0 0.0 copy-done.4
  397.0 1.4 divide_convert_fusion
  (4 shorter events, 0.0 us)
Async XLA Ops:
  7.2 78.4 %all-reduce.6.cloned.1.call-start = ((), (), s32[]{:S(2)}) async-start(), calls=%async_computation | async-start | bytes 4194304 | tf_op jit(solution)/shard_map/psum | solution.py:21
  85.5 1.8 copy-start.1
  85.5 16.9 %copy-start.9 = (f32[256]{0:T(256)S(1)}, f32[256]{0:T(256)}, u32[]{:S(2)}) copy-start(f32[256]{0:T(256)} %param.8) | copy-start | bytes 3076
  85.5 17.0 %copy-start.7 = (f32[1024]{0:T(1024)S(1)}, f32[1024]{0:T(1024)}, u32[]{:S(2)}) copy-start(f32[1024]{0:T(1024)} %param.10) | copy-start | bytes 12292
  85.5 63.7 %copy-start.6 = (f32[2048]{0:T(1024)S(1)}, f32[2048]{0:T(1024)}, u32[]{:S(2)}) copy-start(f32[2048]{0:T(1024)} %param.9) | copy-start | bytes 24580
  87.3 63.4 %copy-start.8 = (f32[512]{0:T(512)S(1)}, f32[512]{0:T(512)}, u32[]{:S(2)}) copy-start(f32[512]{0:T(512)} %param.11) | copy-start | bytes 6148
  87.3 63.4 %copy-start = (bf16[1024,512]{1,0:T(8,128)(2,1)S(1)}, bf16[1024,512]{1,0:T(8,128)(2,1)}, u32[]{:S(2)}) copy-start(bf16[1024,512]{1,0:T(8,128)(2,1)} %get-tuple-element.17) | copy-start | bytes 3145732
  102.5 293.1 %copy-start.5 = (f32[256]{0:T(256)}, f32[256]{0:T(256)S(1)}, u32[]{:S(2)}) copy-start(f32[256]{0:T(256)S(1)} %multiply_add_fusion.3) | copy-start | bytes 3076
  102.5 294.5 %copy-start.3 = (f32[1024]{0:T(1024)}, f32[1024]{0:T(1024)S(1)}, u32[]{:S(2)}) copy-start(f32[1024]{0:T(1024)S(1)} %multiply_add_fusion.1) | copy-start | bytes 12292
  149.2 246.4 %copy-start.2 = (f32[2048]{0:T(1024)}, f32[2048]{0:T(1024)S(1)}, u32[]{:S(2)}) copy-start(f32[2048]{0:T(1024)S(1)} %multiply_add_fusion) | copy-start | bytes 24580
  150.7 246.3 %copy-start.4 = (f32[512]{0:T(512)}, f32[512]{0:T(512)S(1)}, u32[]{:S(2)}) copy-start(f32[512]{0:T(512)S(1)} %multiply_add_fusion.2) | copy-start | bytes 6148
Sparse Core Ops, SparseCore 0:
  10.4 75.0 all-reduce.5
where the time goes:
time: 413 us; the launch traced here: 405 us
  blocking collectives  303 us (73%)
  waiting for transfers between devices  78.3 us (19%)
  between operations  15.5 us (4%)
  other arithmetic  8.11 us (2%)
    psum x1, blocking collectives, local(): lax.psum((local_squares[0], local_squares[1]), ('row', 'col'))  242 us
    psum x1, waiting for transfers between devices, local(): lax.psum(terms[0].astype(jnp.bfloat16), 'dp').astype(jnp.float32)  77.6 us
    psum x1, blocking collectives, column_totals(): lax.psum((jnp.sum(square_wi, axis=0), jnp.sum(square_wo, axis=0)), 'row')  46.7 us
    psum x1, blocking collectives, local(): lax.psum((jnp.sum(square_wi, axis=1), jnp.sum(square_wo, axis=1)), 'col')  14.6 us
  transfers between devices with their start and end apart: 1, of which 1 were waited for; matrix products, arithmetic and copies ran while one was open for 0% of the time, Pallas kernels for 0%

commit v1 on v0

v1 whole, which is shorter than its diff:
```python
import functools

import jax
import jax.numpy as jnp
from jax import lax
from jax.experimental import pallas as pl
from jax.experimental.pallas import tpu as pltpu
from jax.sharding import PartitionSpec as P

BETA = 0.8
EPS_SQUARE = 1e-30
N_DP = 4
HALF = 128
PIECE = 2 * HALF
WIDE = 512
LANES = 128
TILES = WIDE // LANES
ROWS = 64
CHUNKS = HALF // ROWS

MESH = pl.DeviceIdType.MESH
FORWARD, BACKWARD = 0, 1


def kernel(
    n_row,
    n_col,
    grad_wi,
    grad_wo,
    row_wi,
    col_wi,
    row_wo,
    col_wo,
    update_wi,
    row_wi_new,
    col_wi_new,
    update_wo,
    row_wo_new,
    col_wo_new,
    own,
    near,
    passing,
    direct,
    combined,
    total,
    squares,
    row_part,
    col_part,
    z_sums,
    y_sums,
    x_sums,
    row_scale,
    col_scale_wi,
    col_scale_wo,
    z_energy,
    y_energy,
    x_energy,
    load_sem,
    big_send,
    passing_recv,
    direct_recv,
    combined_recv,
    gather_recv,
    onward_recv,
    small_send,
    small_recv,
):
    me = lax.axis_index("dp")
    my_row = lax.axis_index("row")
    my_col = lax.axis_index("col")
    right = lax.rem(me + 1, N_DP)
    left = lax.rem(me + N_DP - 1, N_DP)
    across = lax.rem(me + 2, N_DP)
    target = (right, left)

    def rows_at(c):
        return pl.ds(pl.multiple_of(c * ROWS, ROWS), ROWS)

    def grad_at(m, piece, start, size):
        if m == 0:
            return grad_wi.at[
                0, pl.ds(start, size), pl.ds(pl.multiple_of(piece * WIDE, WIDE), WIDE)
            ]
        return grad_wo.at[
            0, pl.ds(pl.multiple_of(piece * PIECE + start, ROWS), size), :
        ]

    def grad_chunk(m, piece, half, c):
        return grad_at(m, piece, pl.multiple_of(half * HALF + c * ROWS, ROWS), ROWS)

    loads = []
    for m in range(2):
        loads.append(pltpu.make_async_copy(grad_at(m, right, 0, HALF), near.at[FORWARD, m], load_sem.at[m]))
        loads.append(pltpu.make_async_copy(grad_at(m, left, HALF, HALF), near.at[BACKWARD, m], load_sem.at[2 + m]))
        loads.append(pltpu.make_async_copy(grad_at(m, me, 0, PIECE), own.at[m], load_sem.at[4 + m]))
    for load in loads:
        load.start()

    barrier = pltpu.get_barrier_semaphore()

    def greet(axis, n, index):
        def body(d, carry):
            pl.semaphore_signal(
                barrier, inc=1, device_id={axis: lax.rem(index + d, n)}, device_id_type=MESH
            )
            return carry

        lax.fori_loop(1, n, body, 0)

    greet("dp", N_DP, me)
    greet("row", n_row, my_row)
    greet("col", n_col, my_col)
    pl.semaphore_wait(barrier, N_DP + n_row + n_col - 3)

    def send(src, dst, send_sem, recv_sem, to):
        return pltpu.make_async_remote_copy(
            src_ref=src,
            dst_ref=dst,
            send_sem=send_sem,
            recv_sem=recv_sem,
            device_id={"dp": to},
            device_id_type=MESH,
        )

    for m in range(2):

        @pl.loop(0, CHUNKS)
        def _(c):
            for way in (FORWARD, BACKWARD):
                send(
                    grad_chunk(m, across, way, c),
                    passing.at[way, m, rows_at(c)],
                    big_send.at[0],
                    passing_recv.at[way, m, c],
                    target[way],
                ).start()

    for m in range(2):

        @pl.loop(0, CHUNKS)
        def _(c):
            for way in (FORWARD, BACKWARD):
                send(
                    grad_chunk(m, target[way], 1 - way, c),
                    direct.at[way, m, rows_at(c)],
                    big_send.at[1],
                    direct_recv.at[way, m, c],
                    target[way],
                ).start()

    for load in loads:
        load.wait()

    for m in range(2):

        @pl.loop(0, CHUNKS)
        def _(c):
            for way in (FORWARD, BACKWARD):
                here = passing.at[way, m, rows_at(c)]
                send(here, here, big_send.at[0], passing_recv.at[way, m, c], target[way]).wait_recv()
                here[...] = (
                    here[...].astype(jnp.float32) + near[way, m, rows_at(c)].astype(jnp.float32)
                ).astype(jnp.bfloat16)
                send(
                    here,
                    combined.at[way, m, rows_at(c)],
                    big_send.at[2],
                    combined_recv.at[way, m, c],
                    target[way],
                ).start()

    def gather(m, half, c, way):
        part = total.at[me, m, pl.ds(pl.multiple_of(half * HALF + c * ROWS, ROWS), ROWS)]
        return send(part, part, big_send.at[3 + half], gather_recv.at[way, m, half, c], target[way])

    for m in range(2):
        col_part[m] = jnp.zeros((8, WIDE), jnp.float32)

        @pl.loop(0, CHUNKS)
        def _(c):
            for way in (FORWARD, BACKWARD):
                half = way
                first = direct.at[1 - way, m, rows_at(c)]
                second = combined.at[way, m, rows_at(c)]
                send(first, first, big_send.at[1], direct_recv.at[1 - way, m, c], right).wait_recv()
                send(second, second, big_send.at[2], combined_recv.at[way, m, c], right).wait_recv()
                rows = pl.ds(pl.multiple_of(half * HALF + c * ROWS, ROWS), ROWS)
                value = (
                    own[m, rows].astype(jnp.float32)
                    + first[...].astype(jnp.float32)
                    + second[...].astype(jnp.float32)
                )
                total[me, m, rows] = value.astype(jnp.bfloat16)
                gather(m, half, c, way).start()
                square = value * value
                squares[m, rows] = square
                row_part[m, rows] = sum(
                    square[:, k * LANES : (k + 1) * LANES] for k in range(TILES)
                )
                col_part[m] += jnp.sum(square.reshape(ROWS // 8, 8, WIDE), axis=0)

    for m in range(2):

        @pl.loop(0, CHUNKS)
        def _(c):
            for way in (FORWARD, BACKWARD):
                gather(m, 1 - way, c, way).start()

    def exchange_start(buffer, n, axis, index, at):
        def body(d, carry):
            pltpu.make_async_remote_copy(
                src_ref=buffer.at[index],
                dst_ref=buffer.at[index],
                send_sem=small_send.at[at],
                recv_sem=small_recv.at[at],
                device_id={axis: lax.rem(index + d, n)},
                device_id_type=MESH,
            ).start()
            return carry

        lax.fori_loop(1, n, body, 0)

    def exchange_wait(buffer, n, axis, index, at):
        others = buffer.at[pl.ds(0, n - 1)]
        pltpu.make_async_copy(others, others, small_recv.at[at]).wait()
        pltpu.make_async_copy(others, others, small_send.at[at]).wait()

    for m in range(2):
        for half in range(2):
            block = row_part[m, half * HALF : (half + 1) * HALF].T
            z_sums[my_col, m * 2 + half : m * 2 + half + 1] = jnp.sum(block, axis=0, keepdims=True)
    exchange_start(z_sums, n_col, "col", my_col, 0)
    for m in range(2):
        column = jnp.sum(col_part[m], axis=0, keepdims=True)
        for k in range(TILES):
            y_sums[my_row, m * TILES + k : m * TILES + k + 1] = column[:, k * LANES : (k + 1) * LANES]
    exchange_start(y_sums, n_row, "row", my_row, 1)
    exchange_wait(z_sums, n_col, "col", my_col, 0)
    exchange_wait(y_sums, n_row, "row", my_row, 1)

    def add_up(buffer, n):
        result = buffer[0]
        for j in range(1, n):
            result = result + buffer[j]
        return result

    x_sums[me, 0:4] = add_up(z_sums, n_col)
    x_sums[me, 8:16] = add_up(y_sums, n_row)
    exchange_start(x_sums, N_DP, "dp", me, 2)
    exchange_wait(x_sums, N_DP, "dp", me, 2)

    def mix(previous, sums, count):
        return BETA * previous + (1.0 - BETA) * (sums * (1.0 / count) + EPS_SQUARE)

    by_x = [x_sums[x] for x in range(N_DP)]
    rows_wi, rows_wo = n_row * PIECE, n_row * PIECE * N_DP
    cols_wi, cols_wo = n_col * WIDE * N_DP, n_col * WIDE
    new = mix(row_wi[...], by_x[0][0:2] + by_x[1][0:2] + by_x[2][0:2] + by_x[3][0:2], cols_wi)
    row_wi_new[...] = new
    factor_wi = lax.rsqrt(new)
    new = mix(row_wo[...], jnp.concatenate([x[2:4] for x in by_x], axis=0), cols_wo)
    row_wo_new[...] = new
    factor_wo = lax.rsqrt(new)
    for half in range(2):
        row_scale[half] = jnp.broadcast_to(factor_wi[half : half + 1], (LANES, LANES)).T
    for half in range(2 * N_DP):
        row_scale[2 + half] = jnp.broadcast_to(factor_wo[half : half + 1], (LANES, LANES)).T
    new = mix(col_wi[...], jnp.concatenate([x[8:12] for x in by_x], axis=0), rows_wi)
    col_wi_new[...] = new
    col_scale_wi[...] = lax.rsqrt(new)
    new = mix(col_wo[...], by_x[0][12:16] + by_x[1][12:16] + by_x[2][12:16] + by_x[3][12:16], rows_wo)
    col_wo_new[...] = new
    col_scale_wo[...] = lax.rsqrt(new)

    for m in range(2):

        @pl.loop(0, CHUNKS)
        def _(c):
            for way in (FORWARD, BACKWARD):
                source = target[1 - way]
                half = way
                part = total.at[source, m, pl.ds(pl.multiple_of(half * HALF + c * ROWS, ROWS), ROWS)]
                send(part, part, big_send.at[3], gather_recv.at[way, m, half, c], right).wait_recv()
                send(part, part, big_send.at[5], onward_recv.at[way, m, c], target[way]).start()

    for m in range(2):
        energy = jnp.zeros((HALF, LANES), jnp.float32)
        for half in range(2):
            weighted = jnp.zeros((HALF, LANES), jnp.float32)
            for k in range(TILES):
                if m == 0:
                    column = col_scale_wi[pl.ds(me * TILES + k, 1)]
                else:
                    column = col_scale_wo[k : k + 1]
                weighted += squares[m, half * HALF : (half + 1) * HALF, k * LANES : (k + 1) * LANES] * (
                    column * column
                )
            scale = row_scale[half] if m == 0 else row_scale[2 + me * 2 + half]
            energy += weighted * (scale * scale)
        z_energy[my_col, m : m + 1] = jnp.sum(energy, axis=0, keepdims=True)
    exchange_start(z_energy, n_col, "col", my_col, 3)
    exchange_wait(z_energy, n_col, "col", my_col, 3)
    y_energy[my_row] = add_up(z_energy, n_col)
    exchange_start(y_energy, n_row, "row", my_row, 4)
    exchange_wait(y_energy, n_row, "row", my_row, 4)
    x_energy[me] = add_up(y_energy, n_row)
    exchange_start(x_energy, N_DP, "dp", me, 5)
    exchange_wait(x_energy, N_DP, "dp", me, 5)
    energy = jnp.sum(add_up(x_energy, N_DP), axis=1, keepdims=True)
    clip = 1.0 / jnp.maximum(1.0, jnp.sqrt(energy * (1.0 / (rows_wi * cols_wi))))
    col_scale_wi[...] = col_scale_wi[...] * clip[0:1]
    col_scale_wo[...] = col_scale_wo[...] * clip[1:2]

    def finish(piece, m, half, c):
        rows = pl.ds(pl.multiple_of(half * HALF + c * ROWS, ROWS), ROWS)
        value = total[piece, m, rows].astype(jnp.float32)
        if m == 0:
            scale = row_scale[half, rows_at(c)]
        else:
            scale = row_scale[2 + 2 * piece + half, rows_at(c)]
        for k in range(TILES):
            if m == 0:
                column = col_scale_wi[pl.ds(piece * TILES + k, 1)]
            else:
                column = col_scale_wo[k : k + 1]
            result = (value[:, k * LANES : (k + 1) * LANES] * scale * column).astype(jnp.bfloat16)
            if m == 0:
                update_wi[rows, pl.ds(pl.multiple_of(piece * WIDE + k * LANES, LANES), LANES)] = result
            else:
                update_wo[
                    pl.ds(pl.multiple_of(piece * PIECE + half * HALF + c * ROWS, ROWS), ROWS),
                    k * LANES : (k + 1) * LANES,
                ] = result

    for m in range(2):

        @pl.loop(0, CHUNKS)
        def _(c):
            for half in range(2):
                finish(me, m, half, c)

    for m in range(2):

        @pl.loop(0, CHUNKS)
        def _(c):
            for way in (FORWARD, BACKWARD):
                finish(target[1 - way], m, way, c)

    for m in range(2):

        @pl.loop(0, CHUNKS)
        def _(c):
            for way in (FORWARD, BACKWARD):
                source, half = target[1 - way], 1 - way
                part = total.at[source, m, pl.ds(pl.multiple_of(half * HALF + c * ROWS, ROWS), ROWS)]
                send(part, part, big_send.at[3], gather_recv.at[way, m, half, c], right).wait_recv()
                finish(source, m, half, c)

    for m in range(2):

        @pl.loop(0, CHUNKS)
        def _(c):
            for way in (FORWARD, BACKWARD):
                part = total.at[across, m, pl.ds(pl.multiple_of(way * HALF + c * ROWS, ROWS), ROWS)]
                send(part, part, big_send.at[5], onward_recv.at[way, m, c], right).wait_recv()
                finish(across, m, way, c)

    for at in range(6):
        pltpu.make_async_copy(passing, passing, big_send.at[at]).wait()


def local(n_row, n_col, grad_wi, grad_wo, row_wi, col_wi, row_wo, col_wo):
    vmem = pl.BlockSpec(memory_space=pltpu.VMEM)
    hbm = pl.BlockSpec(memory_space=pltpu.HBM)
    f32, bf16 = jnp.float32, jnp.bfloat16

    def folded(x):
        return x.reshape(x.shape[0] // LANES, LANES)

    vectors = [folded(x) for x in (row_wi, col_wi, row_wo, col_wo)]
    out = pl.pallas_call(
        functools.partial(kernel, n_row, n_col),
        out_shape=(
            jax.ShapeDtypeStruct(grad_wi.shape[1:], bf16),
            jax.ShapeDtypeStruct(vectors[0].shape, f32),
            jax.ShapeDtypeStruct(vectors[1].shape, f32),
            jax.ShapeDtypeStruct(grad_wo.shape[1:], bf16),
            jax.ShapeDtypeStruct(vectors[2].shape, f32),
            jax.ShapeDtypeStruct(vectors[3].shape, f32),
        ),
        in_specs=[hbm] * 2 + [vmem] * 4,
        out_specs=[vmem] * 6,
        scratch_shapes=[
            pltpu.VMEM((2, PIECE, WIDE), bf16),
            pltpu.VMEM((2, 2, HALF, WIDE), bf16),
            pltpu.VMEM((2, 2, HALF, WIDE), bf16),
            pltpu.VMEM((2, 2, HALF, WIDE), bf16),
            pltpu.VMEM((2, 2, HALF, WIDE), bf16),
            pltpu.VMEM((N_DP, 2, PIECE, WIDE), bf16),
            pltpu.VMEM((2, PIECE, WIDE), f32),
            pltpu.VMEM((2, PIECE, LANES), f32),
            pltpu.VMEM((2, 8, WIDE), f32),
            pltpu.VMEM((n_col, 4, LANES), f32),
            pltpu.VMEM((n_row, 8, LANES), f32),
            pltpu.VMEM((N_DP, 16, LANES), f32),
            pltpu.VMEM((2 + 2 * N_DP, LANES, LANES), f32),
            pltpu.VMEM(vectors[1].shape, f32),
            pltpu.VMEM(vectors[3].shape, f32),
            pltpu.VMEM((n_col, 2, LANES), f32),
            pltpu.VMEM((n_row, 2, LANES), f32),
            pltpu.VMEM((N_DP, 2, LANES), f32),
            pltpu.SemaphoreType.DMA((6,)),
            pltpu.SemaphoreType.DMA((6,)),
            pltpu.SemaphoreType.DMA((2, 2, CHUNKS)),
            pltpu.SemaphoreType.DMA((2, 2, CHUNKS)),
            pltpu.SemaphoreType.DMA((2, 2, CHUNKS)),
            pltpu.SemaphoreType.DMA((2, 2, 2, CHUNKS)),
            pltpu.SemaphoreType.DMA((2, 2, CHUNKS)),
            pltpu.SemaphoreType.DMA((6,)),
            pltpu.SemaphoreType.DMA((6,)),
        ],
        compiler_params=pltpu.CompilerParams(
            collective_id=0, has_side_effects=True, vmem_limit_bytes=40 * 1024 * 1024
        ),
        name="adafactor",
    )(grad_wi, grad_wo, *vectors)
    return (
        out[0],
        out[1].reshape(row_wi.shape),
        out[2].reshape(col_wi.shape),
        out[3],
        out[4].reshape(row_wo.shape),
        out[5].reshape(col_wo.shape),
    )


def solution(mesh):
    return jax.shard_map(
        functools.partial(local, mesh.shape["row"], mesh.shape["col"]),
        mesh=mesh,
        in_specs=(
            P("dp", "row", "col"),
            P("dp", "row", "col"),
            P("row"),
            P("col"),
            P("row"),
            P("col"),
        ),
        out_specs=(P("row", "col"), P("row"), P("col"), P("row", "col"), P("row"), P("col")),
        check_vma=False,
    )
```

time: 413 us -> 68.8 us (0.17); the launches traced: 405 us -> 68.5 us
  blocking collectives: 303 us -> 0 us
  waiting for transfers between devices: 78.3 us -> 0 us
  Pallas kernels: 0 us -> 59.7 us
  between operations: 15.5 us -> 0.67 us
  other arithmetic: 8.11 us -> 0 us
  local copies, waits for them, and re-layouts: 0.05 us -> 8.11 us
    psum x3 -> x0, blocking collectives: 303 us -> none  [the longest x1 242 us: local(): lax.psum((local_squares[0], local_squares[1]), ('row', 'col'))]
    psum x1 -> x0, waiting for transfers between devices: 77.6 us -> none  [local(): lax.psum(terms[0].astype(jnp.bfloat16), 'dp').astype(jnp.float32)]
    pallas_call x0 -> x1, Pallas kernels: none -> 59.7 us  [local(): pl.pallas_call(functools.partial(kernel, n_row, n_col), out_shape=(jax.Sh...]
    unnamed x20 -> x18, local copies, waits for them, and re-layouts: 0.05 us -> 8.11 us
    reduce_sum x4 -> x0, other arithmetic: 5.26 us -> none  [the longest x2 2.96 us: local(): local_squares = (jnp.sum(raw_wi * raw_wi), jnp.sum(raw_wo * raw_wo))]
  transfers between devices with their start and end apart: 1 -> 0, of which waited for: 1 -> 0; matrix products, arithmetic and copies ran while one was open for 0% -> 0% of each run, Pallas kernels for 0% -> 0%
where the time goes in v1:
time: 68.8 us; the launch traced here: 68.5 us
  Pallas kernels  59.7 us (87%)
  local copies, waits for them, and re-layouts  8.11 us (12%)
    pallas_call x1, Pallas kernels, local(): pl.pallas_call(functools.partial(kernel, n_row, n_col), out_shape=(jax.Sh...  59.7 us
    unnamed x18, local copies, waits for them, and re-layouts  8.11 us

profile of v1, /device:TPU:1, one launch (start us, length us, event | category | flops | bytes accessed | tf_op | source)
XLA Modules:
  0.0 68.5 jit_solution(13219683393723678373)
XLA Ops:
  0.6 0.0 copy-start.3
  0.6 0.0 copy-start.4
  0.7 0.0 copy-start.5
  0.7 0.7 copy-done.3
  1.3 0.0 copy-done.4
  1.3 0.0 copy-done.5
  1.3 0.0 copy-start
  1.3 1.2 %copy-done = bf16[1,256,2048]{2,1,0:T(8,128)(2,1)S(1)} copy-done((bf16[1,256,2048]{2,1,0:T(8,128)(2,1)S(1)}, bf16[1,256,2048]{2,1,0:T(8,128)(2,1)}, u32[]{:S(2)}) %copy-start) | copy-done | bytes 1048600
  2.6 0.0 copy-start.1
  2.6 1.2 %copy-done.1 = bf16[1,1024,512]{2,1,0:T(8,128)(2,1)S(1)} copy-done((bf16[1,1024,512]{2,1,0:T(8,128)(2,1)S(1)}, bf16[1,1024,512]{2,1,0:T(8,128)(2,1)}, u32[]{:S(2)}) %copy-start.1) | copy-done | bytes 1048600
  3.8 0.0 copy-start.2
  3.8 0.7 %copy-done.2 = f32[2048]{0:T(1024)S(1)} copy-done((f32[2048]{0:T(1024)S(1)}, f32[2048]{0:T(1024)}, u32[]{:S(2)}) %copy-start.2) | copy-done | bytes 8216
  4.5 59.7 %adafactor.1 = (bf16[256,2048]{1,0:T(8,128)(2,1)S(1)}, f32[2,128]{1,0:T(2,128)S(1)}, f32[16,128]{1,0:T(8,128)S(1)}, bf16[1024,512]{1,0:T(8,128)(2,1)S(1)}, f32[8,128]{1,0:T(8,128)S(1)}, /*index=5*/f32[4,128]{1,0:T(4,128)S(1)}) custom-call(bf16[1,256,2048]{2,1,0:T(8,128)(2,1)S(1)} %copy-done, bf16[1,1024,512]{2,1,0:T(8,128)(2,1)S(1)} %copy-done.1, ...), custom_call_target="tpu_custom_call" | custom-call | tf_op jit(solution)/shard_map/adafactor/pallas_call | solution.py:381
  64.2 1.0 %copy.18 = bf16[256,2048]{1,0:T(8,128)(2,1)} copy(bf16[256,2048]{1,0:T(8,128)(2,1)S(1)} %get-tuple-element.24) | data formatting | bytes 2097152
  65.2 0.6 copy.19
  65.8 0.6 copy.20
  66.4 1.0 %copy.21 = bf16[1024,512]{1,0:T(8,128)(2,1)} copy(bf16[1024,512]{1,0:T(8,128)(2,1)S(1)} %get-tuple-element.27) | data formatting | bytes 2097152
  67.3 0.6 copy.22
  67.9 0.6 copy.23
Async XLA Ops:
  0.6 0.7 %copy-start.3 = (f32[1024]{0:T(1024)S(1)}, f32[1024]{0:T(1024)}, u32[]{:S(2)}) copy-start(f32[1024]{0:T(1024)} %param.10) | copy-start | bytes 12292
  0.6 0.7 %copy-start.4 = (f32[512]{0:T(512)S(1)}, f32[512]{0:T(512)}, u32[]{:S(2)}) copy-start(f32[512]{0:T(512)} %param.11) | copy-start | bytes 6148
  0.7 0.7 %copy-start.5 = (f32[256]{0:T(256)S(1)}, f32[256]{0:T(256)}, u32[]{:S(2)}) copy-start(f32[256]{0:T(256)} %param.8) | copy-start | bytes 3076
  1.3 1.2 %copy-start = (bf16[1,256,2048]{2,1,0:T(8,128)(2,1)S(1)}, bf16[1,256,2048]{2,1,0:T(8,128)(2,1)}, u32[]{:S(2)}) copy-start(bf16[1,256,2048]{2,1,0:T(8,128)(2,1)} %grad_wi.1) | copy-start | bytes 3145732
  2.6 1.2 %copy-start.1 = (bf16[1,1024,512]{2,1,0:T(8,128)(2,1)S(1)}, bf16[1,1024,512]{2,1,0:T(8,128)(2,1)}, u32[]{:S(2)}) copy-start(bf16[1,1024,512]{2,1,0:T(8,128)(2,1)} %grad_wo.1) | copy-start | bytes 3145732
  3.8 0.7 %copy-start.2 = (f32[2048]{0:T(1024)S(1)}, f32[2048]{0:T(1024)}, u32[]{:S(2)}) copy-start(f32[2048]{0:T(1024)} %param.9) | copy-start | bytes 24580

commit v2 on v1

v2 whole, which is shorter than its diff:
```python
import functools

import jax
import jax.numpy as jnp
from jax import lax
from jax.experimental import pallas as pl
from jax.experimental.pallas import tpu as pltpu
from jax.sharding import PartitionSpec as P

BETA = 0.8
EPS_SQUARE = 1e-30
N_DP = 4
HALF = 128
PIECE = 2 * HALF
WIDE = 512
LANES = 128
TILES = WIDE // LANES
ROWS = 64
CHUNKS = HALF // ROWS

VMEM_LIMIT = 60 * 1024 * 1024

MESH = pl.DeviceIdType.MESH
FORWARD, BACKWARD = 0, 1


def kernel(
    n_row,
    n_col,
    grad_wi,
    grad_wo,
    row_wi_hbm,
    col_wi_hbm,
    row_wo_hbm,
    col_wo_hbm,
    update_wi,
    row_wi_new,
    col_wi_new,
    update_wo,
    row_wo_new,
    col_wo_new,
    row_wi,
    col_wi,
    row_wo,
    col_wo,
    own,
    near,
    passing,
    direct,
    combined,
    total,
    squares,
    row_part,
    col_part,
    y_one,
    z_one,
    z_two,
    x_one,
    y_two,
    x_two,
    y_energy,
    z_energy,
    row_scale,
    col_scale_wi,
    col_scale_wo,
    load_sem,
    big_send,
    passing_recv,
    direct_recv,
    combined_recv,
    gather_recv,
    onward_recv,
    small_send,
    small_recv,
):
    me = lax.axis_index("dp")
    my_row = lax.axis_index("row")
    my_col = lax.axis_index("col")
    right = lax.rem(me + 1, N_DP)
    left = lax.rem(me + N_DP - 1, N_DP)
    across = lax.rem(me + 2, N_DP)
    target = (right, left)

    def rows_at(c):
        return pl.ds(pl.multiple_of(c * ROWS, ROWS), ROWS)

    def grad_at(m, piece, start, size):
        if m == 0:
            return grad_wi.at[
                0, pl.ds(start, size), pl.ds(pl.multiple_of(piece * WIDE, WIDE), WIDE)
            ]
        return grad_wo.at[
            0, pl.ds(pl.multiple_of(piece * PIECE + start, ROWS), size), :
        ]

    def grad_chunk(m, piece, half, c):
        return grad_at(m, piece, pl.multiple_of(half * HALF + c * ROWS, ROWS), ROWS)

    loads = []
    for m in range(2):
        loads.append(pltpu.make_async_copy(grad_at(m, right, 0, HALF), near.at[FORWARD, m], load_sem.at[m]))
        loads.append(pltpu.make_async_copy(grad_at(m, left, HALF, HALF), near.at[BACKWARD, m], load_sem.at[2 + m]))
        loads.append(pltpu.make_async_copy(grad_at(m, me, 0, PIECE), own.at[m], load_sem.at[4 + m]))
    vectors = ((row_wi_hbm, row_wi), (col_wi_hbm, col_wi), (row_wo_hbm, row_wo), (col_wo_hbm, col_wo))
    for at, (source, target_ref) in enumerate(vectors):
        loads.append(pltpu.make_async_copy(source, target_ref, load_sem.at[6 + at]))
    for load in loads:
        load.start()

    barrier = pltpu.get_barrier_semaphore()

    def greet(axis, n, index):
        def body(j, carry):
            step = (j + 1) // 2
            d = n // 2 + step - 2 * step * lax.rem(j, 2)
            pl.semaphore_signal(
                barrier, inc=1, device_id={axis: lax.rem(index + d, n)}, device_id_type=MESH
            )
            return carry

        lax.fori_loop(0, n - 1, body, 0)

    greet("dp", N_DP, me)
    greet("row", n_row, my_row)
    greet("col", n_col, my_col)
    pl.semaphore_wait(barrier, N_DP + n_row + n_col - 3)

    def send(src, dst, send_sem, recv_sem, to):
        return pltpu.make_async_remote_copy(
            src_ref=src,
            dst_ref=dst,
            send_sem=send_sem,
            recv_sem=recv_sem,
            device_id={"dp": to},
            device_id_type=MESH,
        )

    def send_across(m):
        @pl.loop(0, CHUNKS)
        def _(c):
            for way in (FORWARD, BACKWARD):
                send(
                    grad_chunk(m, across, way, c),
                    passing.at[way, m, rows_at(c)],
                    big_send.at[0, m],
                    passing_recv.at[way, m, c],
                    target[way],
                ).start()

    def send_direct(m):
        @pl.loop(0, CHUNKS)
        def _(c):
            for way in (FORWARD, BACKWARD):
                send(
                    grad_chunk(m, target[way], 1 - way, c),
                    direct.at[way, m, rows_at(c)],
                    big_send.at[1, m],
                    direct_recv.at[way, m, c],
                    target[way],
                ).start()

    def send_combined(m):
        @pl.loop(0, CHUNKS)
        def _(c):
            for way in (FORWARD, BACKWARD):
                here = passing.at[way, m, rows_at(c)]
                send(here, here, big_send.at[0, m], passing_recv.at[way, m, c], target[way]).wait_recv()
                here[...] = (
                    here[...].astype(jnp.float32) + near[way, m, rows_at(c)].astype(jnp.float32)
                ).astype(jnp.bfloat16)
                send(
                    here,
                    combined.at[way, m, rows_at(c)],
                    big_send.at[2, m],
                    combined_recv.at[way, m, c],
                    target[way],
                ).start()

    send_across(0)
    send_direct(0)
    send_across(1)
    for load in loads:
        load.wait()
    send_combined(0)
    send_direct(1)
    send_combined(1)

    def gather(m, half, c, way):
        part = total.at[me, m, pl.ds(pl.multiple_of(half * HALF + c * ROWS, ROWS), ROWS)]
        return send(part, part, big_send.at[3 + half, m], gather_recv.at[way, m, half, c], target[way])

    def gather_start(m):
        for second in (0, 1):

            @pl.loop(0, CHUNKS)
            def _(c):
                for way in (FORWARD, BACKWARD):
                    half = 1 - way if second else way
                    gather(m, half, c, way).start()

    def own_totals(m):
        col_part[m] = jnp.zeros((8, WIDE), jnp.float32)

        @pl.loop(0, CHUNKS)
        def _(c):
            for way in (FORWARD, BACKWARD):
                first = direct.at[1 - way, m, rows_at(c)]
                second = combined.at[way, m, rows_at(c)]
                send(first, first, big_send.at[1, m], direct_recv.at[1 - way, m, c], right).wait_recv()
                send(second, second, big_send.at[2, m], combined_recv.at[way, m, c], right).wait_recv()
                rows = pl.ds(pl.multiple_of(way * HALF + c * ROWS, ROWS), ROWS)
                value = (
                    own[m, rows].astype(jnp.float32)
                    + first[...].astype(jnp.float32)
                    + second[...].astype(jnp.float32)
                )
                total[me, m, rows] = value.astype(jnp.bfloat16)
                square = value * value
                squares[m, rows] = square
                row_part[m, rows] = sum(
                    square[:, k * LANES : (k + 1) * LANES] for k in range(TILES)
                )
                col_part[m] += jnp.sum(square.reshape(ROWS // 8, 8, WIDE), axis=0)

    def exchange_start(buffer, n, axis, index, at):
        def body(j, carry):
            step = (j + 1) // 2
            d = n // 2 + step - 2 * step * lax.rem(j, 2)
            pltpu.make_async_remote_copy(
                src_ref=buffer.at[index],
                dst_ref=buffer.at[index],
                send_sem=small_send.at[at],
                recv_sem=small_recv.at[at],
                device_id={axis: lax.rem(index + d, n)},
                device_id_type=MESH,
            ).start()
            return carry

        lax.fori_loop(0, n - 1, body, 0)

    def exchange_wait(buffer, n, axis, index, at):
        others = buffer.at[pl.ds(0, n - 1)]
        pltpu.make_async_copy(others, others, small_recv.at[at]).wait()
        pltpu.make_async_copy(others, others, small_send.at[at]).wait()

    def over_col(buffer, at):
        return buffer, n_col, "col", my_col, at

    def over_row(buffer, at):
        return buffer, n_row, "row", my_row, at

    def over_dp(buffer, at):
        return buffer, N_DP, "dp", me, at

    def add_up(buffer, n):
        result = buffer[0]
        for j in range(1, n):
            result = result + buffer[j]
        return result

    def mix(previous, sums, count):
        return BETA * previous + (1.0 - BETA) * (sums * (1.0 / count) + EPS_SQUARE)

    def down(x):
        return jnp.broadcast_to(x, (LANES, LANES)).T

    def fold_rows(part):
        halves = [part[half * HALF : (half + 1) * HALF].T for half in range(2)]
        return jnp.concatenate([jnp.sum(x, axis=0, keepdims=True) for x in halves], axis=0)

    def row_sums(m):
        return fold_rows(row_part[m])

    def col_sums(m):
        column = jnp.sum(col_part[m], axis=0, keepdims=True)
        return jnp.concatenate([column[:, k * LANES : (k + 1) * LANES] for k in range(TILES)], axis=0)

    def weighted_row_sums(m, inverse):
        return fold_rows(
            sum(squares[m, :, k * LANES : (k + 1) * LANES] * inverse[k : k + 1] for k in range(TILES))
        )

    def weighted_col_sums(m, inverse):
        weights = [down(inverse[half : half + 1]) for half in range(2)]
        result = []
        for k in range(TILES):
            part = jnp.zeros((8, LANES), jnp.float32)
            for half in range(2):
                x = squares[m, half * HALF : (half + 1) * HALF, k * LANES : (k + 1) * LANES] * weights[half]
                part += jnp.sum(x.reshape(HALF // 8, 8, LANES), axis=0)
            result.append(jnp.sum(part, axis=0, keepdims=True))
        return jnp.concatenate(result, axis=0)

    def onward(m):
        @pl.loop(0, CHUNKS)
        def _(c):
            for way in (FORWARD, BACKWARD):
                source = target[1 - way]
                half = way
                part = total.at[source, m, pl.ds(pl.multiple_of(half * HALF + c * ROWS, ROWS), ROWS)]
                send(part, part, big_send.at[3, m], gather_recv.at[way, m, half, c], right).wait_recv()
                send(part, part, big_send.at[5, m], onward_recv.at[way, m, c], target[way]).start()

    rows_wi, rows_wo = n_row * PIECE, n_row * PIECE * N_DP
    cols_wi, cols_wo = n_col * WIDE * N_DP, n_col * WIDE

    own_totals(0)
    y_one[my_row] = col_sums(0)
    exchange_start(*over_row(y_one, 0))
    pltpu.make_async_copy(passing.at[0], passing.at[0], big_send.at[2, 1]).wait()
    gather_start(0)
    own_totals(1)
    z_one[my_col] = row_sums(1)
    exchange_start(*over_col(z_one, 1))
    gather_start(1)

    exchange_wait(*over_row(y_one, 0))
    col_sums_wi = add_up(y_one, n_row)
    own_col_wi = mix(col_wi[pl.ds(me * TILES, TILES)], col_sums_wi, rows_wi)
    z_two[my_col] = jnp.concatenate(
        [row_sums(0), weighted_row_sums(0, 1.0 / own_col_wi)], axis=0
    )
    exchange_start(*over_col(z_two, 2))
    x_one[me] = col_sums_wi
    exchange_start(*over_dp(x_one, 3))
    y_two[my_row, 0:4] = col_sums(1)
    exchange_wait(*over_col(z_one, 1))
    row_sums_wo = add_up(z_one, n_col)
    own_row_wo = mix(row_wo[pl.ds(me * 2, 2)], row_sums_wo, cols_wo)
    y_two[my_row, 4:8] = weighted_col_sums(1, 1.0 / own_row_wo)
    exchange_start(*over_row(y_two, 4))
    exchange_wait(*over_col(z_two, 2))
    x_two[me, 8:12] = add_up(z_two, n_col)
    x_two[me, 12:14] = row_sums_wo
    x_two[me, 14:16] = row_sums_wo
    exchange_wait(*over_row(y_two, 4))
    x_two[me, 0:8] = add_up(y_two, n_row)
    exchange_start(*over_dp(x_two, 5))
    onward(0)
    onward(1)
    exchange_wait(*over_dp(x_two, 5))
    sums = add_up(x_two, N_DP)

    new_row_wi = mix(row_wi[...], sums[8:10], cols_wi)
    energy = jnp.sum(sums[10:12] / new_row_wi, axis=0, keepdims=True)
    y_energy[my_row] = jnp.concatenate([energy, energy], axis=0)
    exchange_start(*over_row(y_energy, 6))
    new_col_wo = mix(col_wo[...], sums[0:4], rows_wo)
    energy = jnp.sum(sums[4:8] / new_col_wo, axis=0, keepdims=True)
    z_energy[my_col] = jnp.concatenate([energy, energy], axis=0)
    exchange_start(*over_col(z_energy, 7))

    row_wi_new[...] = new_row_wi
    factor = lax.rsqrt(new_row_wi)
    for half in range(2):
        row_scale[half] = down(factor[half : half + 1])
    new = mix(row_wo[...], jnp.concatenate([x_two[x, 12:14] for x in range(N_DP)], axis=0), cols_wo)
    row_wo_new[...] = new
    factor = lax.rsqrt(new)
    for half in range(2 * N_DP):
        row_scale[2 + half] = down(factor[half : half + 1])
    exchange_wait(*over_dp(x_one, 3))
    new = mix(col_wi[...], jnp.concatenate([x_one[x] for x in range(N_DP)], axis=0), rows_wi)
    col_wi_new[...] = new
    factor_wi = lax.rsqrt(new)
    col_wo_new[...] = new_col_wo
    factor_wo = lax.rsqrt(new_col_wo)

    def clip(sums):
        energy = jnp.sum(sums[0:1], axis=1, keepdims=True)
        return 1.0 / jnp.maximum(1.0, jnp.sqrt(energy * (1.0 / (rows_wi * cols_wi))))

    exchange_wait(*over_col(z_energy, 7))
    col_scale_wo[...] = factor_wo * clip(add_up(z_energy, n_col))
    exchange_wait(*over_row(y_energy, 6))
    col_scale_wi[...] = factor_wi * clip(add_up(y_energy, n_row))

    def finish(piece, m, half, c):
        rows = pl.ds(pl.multiple_of(half * HALF + c * ROWS, ROWS), ROWS)
        value = total[piece, m, rows].astype(jnp.float32)
        if m == 0:
            scale = row_scale[half, rows_at(c)]
        else:
            scale = row_scale[2 + 2 * piece + half, rows_at(c)]
        for k in range(TILES):
            if m == 0:
                column = col_scale_wi[pl.ds(piece * TILES + k, 1)]
            else:
                column = col_scale_wo[k : k + 1]
            result = (value[:, k * LANES : (k + 1) * LANES] * scale * column).astype(jnp.bfloat16)
            if m == 0:
                update_wi[rows, pl.ds(pl.multiple_of(piece * WIDE + k * LANES, LANES), LANES)] = result
            else:
                update_wo[
                    pl.ds(pl.multiple_of(piece * PIECE + half * HALF + c * ROWS, ROWS), ROWS),
                    k * LANES : (k + 1) * LANES,
                ] = result

    for m in range(2):

        @pl.loop(0, CHUNKS)
        def _(c):
            for half in range(2):
                finish(me, m, half, c)

    for m in range(2):

        @pl.loop(0, CHUNKS)
        def _(c):
            for way in (FORWARD, BACKWARD):
                finish(target[1 - way], m, way, c)

    for m in range(2):

        @pl.loop(0, CHUNKS)
        def _(c):
            for way in (FORWARD, BACKWARD):
                source, half = target[1 - way], 1 - way
                part = total.at[source, m, pl.ds(pl.multiple_of(half * HALF + c * ROWS, ROWS), ROWS)]
                send(part, part, big_send.at[3, m], gather_recv.at[way, m, half, c], right).wait_recv()
                finish(source, m, half, c)

    for m in range(2):

        @pl.loop(0, CHUNKS)
        def _(c):
            for way in (FORWARD, BACKWARD):
                part = total.at[across, m, pl.ds(pl.multiple_of(way * HALF + c * ROWS, ROWS), ROWS)]
                send(part, part, big_send.at[5, m], onward_recv.at[way, m, c], right).wait_recv()
                finish(across, m, way, c)

    for at in range(6):
        for m in range(2):
            if (at, m) != (2, 1):
                pltpu.make_async_copy(passing.at[0], passing.at[0], big_send.at[at, m]).wait()


def write_back(*refs):
    sources, results, sem = refs[:6], refs[6:12], refs[12]
    copies = [pltpu.make_async_copy(a, b, sem.at[i]) for i, (a, b) in enumerate(zip(sources, results))]
    for copy in copies:
        copy.start()
    for copy in copies:
        copy.wait()


def local(n_row, n_col, grad_wi, grad_wo, row_wi, col_wi, row_wo, col_wo):
    vmem = pl.BlockSpec(memory_space=pltpu.VMEM)
    hbm = pl.BlockSpec(memory_space=pltpu.HBM)
    f32, bf16 = jnp.float32, jnp.bfloat16

    def folded(x):
        return x.reshape(x.shape[0] // LANES, LANES)

    vectors = [folded(x) for x in (row_wi, col_wi, row_wo, col_wo)]
    out = pl.pallas_call(
        functools.partial(kernel, n_row, n_col),
        out_shape=(
            pltpu.VMEM(grad_wi.shape[1:], bf16),
            pltpu.VMEM(vectors[0].shape, f32),
            pltpu.VMEM(vectors[1].shape, f32),
            pltpu.VMEM(grad_wo.shape[1:], bf16),
            pltpu.VMEM(vectors[2].shape, f32),
            pltpu.VMEM(vectors[3].shape, f32),
        ),
        in_specs=[hbm] * 6,
        out_specs=[vmem] * 6,
        scratch_shapes=[pltpu.VMEM(x.shape, f32) for x in vectors]
        + [
            pltpu.VMEM((2, PIECE, WIDE), bf16),
            pltpu.VMEM((2, 2, HALF, WIDE), bf16),
            pltpu.VMEM((2, 2, HALF, WIDE), bf16),
            pltpu.VMEM((2, 2, HALF, WIDE), bf16),
            pltpu.VMEM((2, 2, HALF, WIDE), bf16),
            pltpu.VMEM((N_DP, 2, PIECE, WIDE), bf16),
            pltpu.VMEM((2, PIECE, WIDE), f32),
            pltpu.VMEM((2, PIECE, LANES), f32),
            pltpu.VMEM((2, 8, WIDE), f32),
            pltpu.VMEM((n_row, 4, LANES), f32),
            pltpu.VMEM((n_col, 2, LANES), f32),
            pltpu.VMEM((n_col, 4, LANES), f32),
            pltpu.VMEM((N_DP, 4, LANES), f32),
            pltpu.VMEM((n_row, 8, LANES), f32),
            pltpu.VMEM((N_DP, 16, LANES), f32),
            pltpu.VMEM((n_row, 2, LANES), f32),
            pltpu.VMEM((n_col, 2, LANES), f32),
            pltpu.VMEM((2 + 2 * N_DP, LANES, LANES), f32),
            pltpu.VMEM(vectors[1].shape, f32),
            pltpu.VMEM(vectors[3].shape, f32),
            pltpu.SemaphoreType.DMA((10,)),
            pltpu.SemaphoreType.DMA((6, 2)),
            pltpu.SemaphoreType.DMA((2, 2, CHUNKS)),
            pltpu.SemaphoreType.DMA((2, 2, CHUNKS)),
            pltpu.SemaphoreType.DMA((2, 2, CHUNKS)),
            pltpu.SemaphoreType.DMA((2, 2, 2, CHUNKS)),
            pltpu.SemaphoreType.DMA((2, 2, CHUNKS)),
            pltpu.SemaphoreType.DMA((8,)),
            pltpu.SemaphoreType.DMA((8,)),
        ],
        compiler_params=pltpu.CompilerParams(
            collective_id=0, has_side_effects=True, vmem_limit_bytes=VMEM_LIMIT
        ),
        name="adafactor",
    )(grad_wi, grad_wo, *vectors)
    out = pl.pallas_call(
        write_back,
        out_shape=tuple(jax.ShapeDtypeStruct(x.shape, x.dtype) for x in out),
        in_specs=[vmem] * 6,
        out_specs=[hbm] * 6,
        scratch_shapes=[pltpu.SemaphoreType.DMA((6,))],
        compiler_params=pltpu.CompilerParams(vmem_limit_bytes=2 * 1024 * 1024),
        name="write_back",
    )(*[pltpu.with_memory_space_constraint(x, pltpu.VMEM) for x in out])
    return (
        out[0],
        out[1].reshape(row_wi.shape),
        out[2].reshape(col_wi.shape),
        out[3],
        out[4].reshape(row_wo.shape),
        out[5].reshape(col_wo.shape),
    )


def solution(mesh):
    return jax.shard_map(
        functools.partial(local, mesh.shape["row"], mesh.shape["col"]),
        mesh=mesh,
        in_specs=(
            P("dp", "row", "col"),
            P("dp", "row", "col"),
            P("row"),
            P("col"),
            P("row"),
            P("col"),
        ),
        out_specs=(P("row", "col"), P("row"), P("col"), P("row", "col"), P("row"), P("col")),
        check_vma=False,
    )
```

time: 68.8 us -> 55.6 us (0.81)
  local copies, waits for them, and re-layouts: 8.11 us -> 0 us
  Pallas kernels: 59.7 us -> 54.9 us
    unnamed x18 -> x0, local copies, waits for them, and re-layouts: 8.11 us -> none
    pallas_call x1 -> x2, Pallas kernels: 59.7 us -> 54.9 us  [the longest x1 53.5 us: local(): pl.pallas_call(functools.partial(kernel, n_row, n_col), out_shape=(pltpu....]
where the time goes in v2:
time: 55.6 us; the launch traced here: 55.5 us
  Pallas kernels  54.9 us (99%)
  between operations  0.64 us (1%)
    pallas_call x1, Pallas kernels, local(): pl.pallas_call(functools.partial(kernel, n_row, n_col), out_shape=(pltpu....  53.5 us
    pallas_call x1, Pallas kernels, local(): pl.pallas_call(write_back, out_shape=tuple((jax.ShapeDtypeStruct(x.shape,...  1.38 us

profile of v2, /device:TPU:1, one launch (start us, length us, event | category | flops | bytes accessed | tf_op | source)
XLA Modules:
  0.0 55.5 jit_solution(7688617620709460664)
XLA Ops:
  0.6 53.5 %adafactor.1 = (bf16[256,2048]{1,0:T(8,128)(2,1)S(1)}, f32[2,128]{1,0:T(2,128)S(1)}, f32[16,128]{1,0:T(8,128)S(1)}, bf16[1024,512]{1,0:T(8,128)(2,1)S(1)}, f32[8,128]{1,0:T(8,128)S(1)}, /*index=5*/f32[4,128]{1,0:T(4,128)S(1)}) custom-call(bf16[1,256,2048]{2,1,0:T(8,128)(2,1)} %grad_wi.1, bf16[1,1024,512]{2,1,0:T(8,128)(2,1)} %grad_wo.1, f32[2,128]{1,0:T(2,128)} %bitcast.11, ...), custom_call_target="tpu_custom_call" | custom-call | tf_op jit(solution)/shard_map/adafactor/pallas_call | solution.py:456
  54.1 1.4 %write_back.1 = (bf16[256,2048]{1,0:T(8,128)(2,1)}, f32[2,128]{1,0:T(2,128)}, f32[16,128]{1,0:T(8,128)}, bf16[1024,512]{1,0:T(8,128)(2,1)}, f32[8,128]{1,0:T(8,128)}, /*index=5*/f32[4,128]{1,0:T(4,128)}) custom-call(bf16[256,2048]{1,0:T(8,128)(2,1)S(1)} %get-tuple-element.18.refs_0_, f32[2,128]{1,0:T(2,128)S(1)} %get-tuple-element.19.refs_1_, ...), custom_call_target="tpu_custom_call" | custom-call | tf_op jit(solution)/shard_map/write_back/pallas_call | solution.py:505

commit v3 on v2

--- a/solution.py
+++ b/solution.py
@@ -15,7 +15,7 @@
 WIDE = 512
 LANES = 128
 TILES = WIDE // LANES
-ROWS = 64
+ROWS = 128
 CHUNKS = HALF // ROWS
 
 VMEM_LIMIT = 60 * 1024 * 1024
@@ -33,10 +33,12 @@
     col_wi_hbm,
     row_wo_hbm,
     col_wo_hbm,
-    update_wi,
+    total,
+    row_scale,
+    col_scale_wi,
+    col_scale_wo,
     row_wi_new,
     col_wi_new,
-    update_wo,
     row_wo_new,
     col_wo_new,
     row_wi,
@@ -48,7 +50,6 @@
     passing,
     direct,
     combined,
-    total,
     squares,
     row_part,
     col_part,
@@ -58,11 +59,10 @@
     x_one,
     y_two,
     x_two,
+    x_three,
     y_energy,
     z_energy,
-    row_scale,
-    col_scale_wi,
-    col_scale_wo,
+    ready,
     load_sem,
     big_send,
     passing_recv,
@@ -109,21 +109,38 @@
 
     barrier = pltpu.get_barrier_semaphore()
 
-    def greet(axis, n, index):
-        def body(j, carry):
-            step = (j + 1) // 2
-            d = n // 2 + step - 2 * step * lax.rem(j, 2)
-            pl.semaphore_signal(
-                barrier, inc=1, device_id={axis: lax.rem(index + d, n)}, device_id_type=MESH
-            )
-            return carry
-
-        lax.fori_loop(0, n - 1, body, 0)
-
-    greet("dp", N_DP, me)
-    greet("row", n_row, my_row)
-    greet("col", n_col, my_col)
-    pl.semaphore_wait(barrier, N_DP + n_row + n_col - 3)
+    n_y = n_row // 2
+    core = lax.rem(my_row, 2)
+
+    def beside(n):
+        return [] if n == 1 else [1] if n == 2 else [1, n - 1]
+
+    def signal(sem, axis, n, index, d):
+        pl.semaphore_signal(
+            sem, inc=1, device_id={axis: lax.rem(index + d, n)}, device_id_type=MESH
+        )
+
+    near_row = [2 * d for d in beside(n_y)]
+    near_col = beside(n_col)
+    for d in range(1, N_DP):
+        signal(barrier, "dp", N_DP, me, d)
+    for d in near_row:
+        signal(barrier, "row", n_row, my_row, d)
+    for d in near_col:
+        signal(barrier, "col", n_col, my_col, d)
+    pl.semaphore_signal(barrier, inc=1, device_id={"row": my_row + 1 - 2 * core}, device_id_type=MESH)
+    pl.semaphore_wait(barrier, N_DP + len(near_row) + len(near_col))
+
+    def tell(at):
+        for d in near_row:
+            signal(ready.at[0, at], "row", n_row, my_row, d)
+        for d in near_col:
+            signal(ready.at[1, at], "col", n_col, my_col, d)
+
+    def hear(at):
+        for axis, count in ((0, len(near_row)), (1, len(near_col))):
+            if count:
+                pl.semaphore_wait(ready.at[axis, at], count)
 
     def send(src, dst, send_sem, recv_sem, to):
         return pltpu.make_async_remote_copy(
@@ -179,11 +196,18 @@
     send_across(0)
     send_direct(0)
     send_across(1)
+    tell(0)
     for load in loads:
         load.wait()
+    hear(0)
+    tell(1)
     send_combined(0)
     send_direct(1)
+    hear(1)
+    tell(2)
     send_combined(1)
+    hear(2)
+    tell(3)
 
     def gather(m, half, c, way):
         part = total.at[me, m, pl.ds(pl.multiple_of(half * HALF + c * ROWS, ROWS), ROWS)]
@@ -305,6 +329,7 @@
     cols_wi, cols_wo = n_col * WIDE * N_DP, n_col * WIDE
 
     own_totals(0)
+    hear(3)
     y_one[my_row] = col_sums(0)
     exchange_start(*over_row(y_one, 0))
     pltpu.make_async_copy(passing.at[0], passing.at[0], big_send.at[2, 1]).wait()
@@ -321,30 +346,31 @@
         [row_sums(0), weighted_row_sums(0, 1.0 / own_col_wi)], axis=0
     )
     exchange_start(*over_col(z_two, 2))
-    x_one[me] = col_sums_wi
-    exchange_start(*over_dp(x_one, 3))
     y_two[my_row, 0:4] = col_sums(1)
     exchange_wait(*over_col(z_one, 1))
     row_sums_wo = add_up(z_one, n_col)
     own_row_wo = mix(row_wo[pl.ds(me * 2, 2)], row_sums_wo, cols_wo)
     y_two[my_row, 4:8] = weighted_col_sums(1, 1.0 / own_row_wo)
     exchange_start(*over_row(y_two, 4))
+
     exchange_wait(*over_col(z_two, 2))
-    x_two[me, 8:12] = add_up(z_two, n_col)
-    x_two[me, 12:14] = row_sums_wo
-    x_two[me, 14:16] = row_sums_wo
+    x_one[me] = jnp.concatenate([add_up(z_two, n_col), col_sums_wi], axis=0)
+    exchange_start(*over_dp(x_one, 3))
     exchange_wait(*over_row(y_two, 4))
-    x_two[me, 0:8] = add_up(y_two, n_row)
+    x_two[me] = add_up(y_two, n_row)
     exchange_start(*over_dp(x_two, 5))
+    x_three[me] = row_sums_wo
+    exchange_start(*over_dp(x_three, 8))
     onward(0)
     onward(1)
+    exchange_wait(*over_dp(x_one, 3))
+    sums = x_one[0, 0:4] + x_one[1, 0:4] + x_one[2, 0:4] + x_one[3, 0:4]
+    new_row_wi = mix(row_wi[...], sums[0:2], cols_wi)
+    energy = jnp.sum(sums[2:4] / new_row_wi, axis=0, keepdims=True)
+    y_energy[my_row] = jnp.concatenate([energy, energy], axis=0)
+    exchange_start(*over_row(y_energy, 6))
     exchange_wait(*over_dp(x_two, 5))
     sums = add_up(x_two, N_DP)
-
-    new_row_wi = mix(row_wi[...], sums[8:10], cols_wi)
-    energy = jnp.sum(sums[10:12] / new_row_wi, axis=0, keepdims=True)
-    y_energy[my_row] = jnp.concatenate([energy, energy], axis=0)
-    exchange_start(*over_row(y_energy, 6))
     new_col_wo = mix(col_wo[...], sums[0:4], rows_wo)
     energy = jnp.sum(sums[4:8] / new_col_wo, axis=0, keepdims=True)
     z_energy[my_col] = jnp.concatenate([energy, energy], axis=0)
@@ -354,13 +380,13 @@
     factor = lax.rsqrt(new_row_wi)
     for half in range(2):
         row_scale[half] = down(factor[half : half + 1])
-    new = mix(row_wo[...], jnp.concatenate([x_two[x, 12:14] for x in range(N_DP)], axis=0), cols_wo)
+    exchange_wait(*over_dp(x_three, 8))
+    new = mix(row_wo[...], jnp.concatenate([x_three[x] for x in range(N_DP)], axis=0), cols_wo)
     row_wo_new[...] = new
     factor = lax.rsqrt(new)
     for half in range(2 * N_DP):
         row_scale[2 + half] = down(factor[half : half + 1])
-    exchange_wait(*over_dp(x_one, 3))
-    new = mix(col_wi[...], jnp.concatenate([x_one[x] for x in range(N_DP)], axis=0), rows_wi)
+    new = mix(col_wi[...], jnp.concatenate([x_one[x, 4:8] for x in range(N_DP)], axis=0), rows_wi)
     col_wi_new[...] = new
     factor_wi = lax.rsqrt(new)
     col_wo_new[...] = new_col_wo
@@ -370,64 +396,21 @@
         energy = jnp.sum(sums[0:1], axis=1, keepdims=True)
         return 1.0 / jnp.maximum(1.0, jnp.sqrt(energy * (1.0 / (rows_wi * cols_wi))))
 
+    exchange_wait(*over_row(y_energy, 6))
+    col_scale_wi[...] = factor_wi * clip(add_up(y_energy, n_row))
     exchange_wait(*over_col(z_energy, 7))
     col_scale_wo[...] = factor_wo * clip(add_up(z_energy, n_col))
-    exchange_wait(*over_row(y_energy, 6))
-    col_scale_wi[...] = factor_wi * clip(add_up(y_energy, n_row))
-
-    def finish(piece, m, half, c):
-        rows = pl.ds(pl.multiple_of(half * HALF + c * ROWS, ROWS), ROWS)
-        value = total[piece, m, rows].astype(jnp.float32)
-        if m == 0:
-            scale = row_scale[half, rows_at(c)]
-        else:
-            scale = row_scale[2 + 2 * piece + half, rows_at(c)]
-        for k in range(TILES):
-            if m == 0:
-                column = col_scale_wi[pl.ds(piece * TILES + k, 1)]
-            else:
-                column = col_scale_wo[k : k + 1]
-            result = (value[:, k * LANES : (k + 1) * LANES] * scale * column).astype(jnp.bfloat16)
-            if m == 0:
-                update_wi[rows, pl.ds(pl.multiple_of(piece * WIDE + k * LANES, LANES), LANES)] = result
-            else:
-                update_wo[
-                    pl.ds(pl.multiple_of(piece * PIECE + half * HALF + c * ROWS, ROWS), ROWS),
-                    k * LANES : (k + 1) * LANES,
-                ] = result
-
-    for m in range(2):
-
-        @pl.loop(0, CHUNKS)
-        def _(c):
-            for half in range(2):
-                finish(me, m, half, c)
 
     for m in range(2):
 
         @pl.loop(0, CHUNKS)
         def _(c):
             for way in (FORWARD, BACKWARD):
-                finish(target[1 - way], m, way, c)
-
-    for m in range(2):
-
-        @pl.loop(0, CHUNKS)
-        def _(c):
-            for way in (FORWARD, BACKWARD):
-                source, half = target[1 - way], 1 - way
-                part = total.at[source, m, pl.ds(pl.multiple_of(half * HALF + c * ROWS, ROWS), ROWS)]
+                half = 1 - way
+                part = total.at[target[1 - way], m, pl.ds(pl.multiple_of(half * HALF + c * ROWS, ROWS), ROWS)]
                 send(part, part, big_send.at[3, m], gather_recv.at[way, m, half, c], right).wait_recv()
-                finish(source, m, half, c)
-
-    for m in range(2):
-
-        @pl.loop(0, CHUNKS)
-        def _(c):
-            for way in (FORWARD, BACKWARD):
                 part = total.at[across, m, pl.ds(pl.multiple_of(way * HALF + c * ROWS, ROWS), ROWS)]
                 send(part, part, big_send.at[5, m], onward_recv.at[way, m, c], right).wait_recv()
-                finish(across, m, way, c)
 
     for at in range(6):
         for m in range(2):
@@ -435,13 +418,79 @@
                 pltpu.make_async_copy(passing.at[0], passing.at[0], big_send.at[at, m]).wait()
 
 
-def write_back(*refs):
-    sources, results, sem = refs[:6], refs[6:12], refs[12]
-    copies = [pltpu.make_async_copy(a, b, sem.at[i]) for i, (a, b) in enumerate(zip(sources, results))]
-    for copy in copies:
+def finish(
+    total,
+    row_scale,
+    col_scale_wi,
+    col_scale_wo,
+    row_wi_new,
+    col_wi_new,
+    row_wo_new,
+    col_wo_new,
+    update_wi,
+    row_wi_out,
+    col_wi_out,
+    update_wo,
+    row_wo_out,
+    col_wo_out,
+    ready_wi,
+    ready_wo,
+    small_sem,
+    big_sem,
+):
+    small = [
+        pltpu.make_async_copy(source, result, small_sem.at[at])
+        for at, (source, result) in enumerate(
+            (
+                (row_wi_new, row_wi_out),
+                (col_wi_new, col_wi_out),
+                (row_wo_new, row_wo_out),
+                (col_wo_new, col_wo_out),
+            )
+        )
+    ]
+    for copy in small:
         copy.start()
-    for copy in copies:
+
+    def block(m, piece, half):
+        if m == 0:
+            at = (
+                pl.ds(pl.multiple_of(half * HALF, HALF), HALF),
+                pl.ds(pl.multiple_of(piece * WIDE, WIDE), WIDE),
+            )
+            return ready_wi.at[at], update_wi.at[at]
+        at = pl.ds(pl.multiple_of(piece * PIECE + half * HALF, HALF), HALF)
+        return ready_wo.at[at], update_wo.at[at]
+
+    def write(m, piece, half):
+        source, result = block(m, piece, half)
+        return pltpu.make_async_copy(source, result, big_sem.at[m, piece, half])
+
+    for m in range(2):
+
+        @pl.loop(0, 2 * N_DP)
+        def _(step):
+            piece, half = step // 2, step % 2
+            ready = block(m, piece, half)[0]
+            rows = pl.ds(pl.multiple_of(half * HALF, HALF), HALF)
+            value = total[piece, m, rows].astype(jnp.float32)
+            scale = row_scale[half] if m == 0 else row_scale[2 + step]
+            for k in range(TILES):
+                if m == 0:
+                    column = col_scale_wi[pl.ds(piece * TILES + k, 1)]
+                else:
+                    column = col_scale_wo[k : k + 1]
+                part = slice(k * LANES, (k + 1) * LANES)
+                ready[:, part] = (value[:, part] * scale * column).astype(jnp.bfloat16)
+            write(m, piece, half).start()
+
+    for copy in small:
         copy.wait()
+    for m in range(2):
+
+        @pl.loop(0, 2 * N_DP)
+        def _(step):
+            write(m, step // 2, step % 2).wait()
 
 
 def local(n_row, n_col, grad_wi, grad_wo, row_wi, col_wi, row_wo, col_wo):
@@ -456,15 +505,14 @@
     out = pl.pallas_call(
         functools.partial(kernel, n_row, n_col),
         out_shape=(
-            pltpu.VMEM(grad_wi.shape[1:], bf16),
-            pltpu.VMEM(vectors[0].shape, f32),
+            pltpu.VMEM((N_DP, 2, PIECE, WIDE), bf16),
+            pltpu.VMEM((2 + 2 * N_DP, LANES, LANES), f32),
             pltpu.VMEM(vectors[1].shape, f32),
-            pltpu.VMEM(grad_wo.shape[1:], bf16),
-            pltpu.VMEM(vectors[2].shape, f32),
             pltpu.VMEM(vectors[3].shape, f32),
-        ),
+        )
+        + tuple(pltpu.VMEM(x.shape, f32) for x in vectors),
         in_specs=[hbm] * 6,
-        out_specs=[vmem] * 6,
+        out_specs=[vmem] * 8,
         scratch_shapes=[pltpu.VMEM(x.shape, f32) for x in vectors]
         + [
             pltpu.VMEM((2, PIECE, WIDE), bf16),
@@ -472,21 +520,19 @@
             pltpu.VMEM((2, 2, HALF, WIDE), bf16),
             pltpu.VMEM((2, 2, HALF, WIDE), bf16),
             pltpu.VMEM((2, 2, HALF, WIDE), bf16),
-            pltpu.VMEM((N_DP, 2, PIECE, WIDE), bf16),
             pltpu.VMEM((2, PIECE, WIDE), f32),
             pltpu.VMEM((2, PIECE, LANES), f32),
             pltpu.VMEM((2, 8, WIDE), f32),
             pltpu.VMEM((n_row, 4, LANES), f32),
             pltpu.VMEM((n_col, 2, LANES), f32),
             pltpu.VMEM((n_col, 4, LANES), f32),
-            pltpu.VMEM((N_DP, 4, LANES), f32),
+            pltpu.VMEM((N_DP, 8, LANES), f32),
             pltpu.VMEM((n_row, 8, LANES), f32),
-            pltpu.VMEM((N_DP, 16, LANES), f32),
+            pltpu.VMEM((N_DP, 8, LANES), f32),
+            pltpu.VMEM((N_DP, 2, LANES), f32),
             pltpu.VMEM((n_row, 2, LANES), f32),
             pltpu.VMEM((n_col, 2, LANES), f32),
-            pltpu.VMEM((2 + 2 * N_DP, LANES, LANES), f32),
-            pltpu.VMEM(vectors[1].shape, f32),
-            pltpu.VMEM(vectors[3].shape, f32),
+            pltpu.SemaphoreType.REGULAR((2, 4)),
             pltpu.SemaphoreType.DMA((10,)),
             pltpu.SemaphoreType.DMA((6, 2)),
             pltpu.SemaphoreType.DMA((2, 2, CHUNKS)),
@@ -494,8 +540,8 @@
             pltpu.SemaphoreType.DMA((2, 2, CHUNKS)),
             pltpu.SemaphoreType.DMA((2, 2, 2, CHUNKS)),
             pltpu.SemaphoreType.DMA((2, 2, CHUNKS)),
-            pltpu.SemaphoreType.DMA((8,)),
-            pltpu.SemaphoreType.DMA((8,)),
+            pltpu.SemaphoreType.DMA((9,)),
+            pltpu.SemaphoreType.DMA((9,)),
         ],
         compiler_params=pltpu.CompilerParams(
             collective_id=0, has_side_effects=True, vmem_limit_bytes=VMEM_LIMIT
@@ -503,13 +549,25 @@
         name="adafactor",
     )(grad_wi, grad_wo, *vectors)
     out = pl.pallas_call(
-        write_back,
-        out_shape=tuple(jax.ShapeDtypeStruct(x.shape, x.dtype) for x in out),
-        in_specs=[vmem] * 6,
+        finish,
+        out_shape=(
+            jax.ShapeDtypeStruct(grad_wi.shape[1:], bf16),
+            jax.ShapeDtypeStruct(vectors[0].shape, f32),
+            jax.ShapeDtypeStruct(vectors[1].shape, f32),
+            jax.ShapeDtypeStruct(grad_wo.shape[1:], bf16),
+            jax.ShapeDtypeStruct(vectors[2].shape, f32),
+            jax.ShapeDtypeStruct(vectors[3].shape, f32),
+        ),
+        in_specs=[vmem] * 8,
         out_specs=[hbm] * 6,
-        scratch_shapes=[pltpu.SemaphoreType.DMA((6,))],
-        compiler_params=pltpu.CompilerParams(vmem_limit_bytes=2 * 1024 * 1024),
-        name="write_back",
+        scratch_shapes=[
+            pltpu.VMEM(grad_wi.shape[1:], bf16),
+            pltpu.VMEM(grad_wo.shape[1:], bf16),
+            pltpu.SemaphoreType.DMA((4,)),
+            pltpu.SemaphoreType.DMA((2, N_DP, 2)),
+        ],
+        compiler_params=pltpu.CompilerParams(vmem_limit_bytes=6 * 1024 * 1024),
+        name="finish",
     )(*[pltpu.with_memory_space_constraint(x, pltpu.VMEM) for x in out])
     return (
         out[0],

time: 55.6 us -> 54.8 us (0.986)
  Pallas kernels: 54.9 us -> 54.1 us
    pallas_call x1, Pallas kernels: 53.5 us -> 52.5 us  [local(): pl.pallas_call(functools.partial(kernel, n_row, n_col), out_shape=(pltpu....]
where the time goes in v3:
time: 54.8 us; the launch traced here: 54.7 us
  Pallas kernels  54.1 us (99%)
  between operations  0.64 us (1%)
    pallas_call x1, Pallas kernels, local(): pl.pallas_call(functools.partial(kernel, n_row, n_col), out_shape=(pltpu....  52.5 us
    pallas_call x1, Pallas kernels, local(): pl.pallas_call(finish, out_shape=(jax.ShapeDtypeStruct(grad_wi.shape[1:],...  1.57 us

profile of v3, /device:TPU:1, one launch (start us, length us, event | category | flops | bytes accessed | tf_op | source)
XLA Modules:
  0.0 54.7 jit_solution(7141727903158343897)
XLA Ops:
  0.6 52.5 %adafactor.1 = (bf16[4,2,256,512]{3,2,1,0:T(8,128)(2,1)S(1)}, f32[10,128,128]{2,1,0:T(8,128)S(1)}, f32[16,128]{1,0:T(8,128)S(1)}, f32[4,128]{1,0:T(4,128)S(1)}, ...) custom-call(bf16[1,256,2048]{2,1,0:T(8,128)(2,1)} %grad_wi.1, ...), custom_call_target="tpu_custom_call" | custom-call | tf_op jit(solution)/shard_map/adafactor/pallas_call | solution.py:505
  53.1 1.6 %finish.1 = (bf16[256,2048]{1,0:T(8,128)(2,1)}, f32[2,128]{1,0:T(2,128)}, f32[16,128]{1,0:T(8,128)}, bf16[1024,512]{1,0:T(8,128)(2,1)}, f32[8,128]{1,0:T(8,128)}, /*index=5*/f32[4,128]{1,0:T(4,128)}) custom-call(bf16[4,2,256,512]{3,2,1,0:T(8,128)(2,1)S(1)} %get-tuple-element.20.total, f32[10,128,128]{2,1,0:T(8,128)S(1)} %get-tuple-element.21.row_scale, ...), custom_call_target="tpu_custom_call" | custom-call | tf_op jit(solution)/shard_map/finish/pallas_call | solution.py:551

commit v4 on v3

--- a/solution.py
+++ b/solution.py
@@ -196,18 +196,11 @@
     send_across(0)
     send_direct(0)
     send_across(1)
-    tell(0)
     for load in loads:
         load.wait()
-    hear(0)
-    tell(1)
     send_combined(0)
     send_direct(1)
-    hear(1)
-    tell(2)
     send_combined(1)
-    hear(2)
-    tell(3)
 
     def gather(m, half, c, way):
         part = total.at[me, m, pl.ds(pl.multiple_of(half * HALF + c * ROWS, ROWS), ROWS)]
@@ -328,6 +321,13 @@
     rows_wi, rows_wo = n_row * PIECE, n_row * PIECE * N_DP
     cols_wi, cols_wo = n_col * WIDE * N_DP, n_col * WIDE
 
+    tell(0)
+    hear(0)
+    tell(1)
+    hear(1)
+    tell(2)
+    hear(2)
+    tell(3)
     own_totals(0)
     hear(3)
     y_one[my_row] = col_sums(0)

time: 54.8 us -> 53.9 us (0.984)
  Pallas kernels: 54.1 us -> 53.2 us
    pallas_call x1, Pallas kernels: 52.5 us -> 51.6 us  [local(): pl.pallas_call(functools.partial(kernel, n_row, n_col), out_shape=(pltpu....]
where the time goes in v4:
time: 53.9 us; the launch traced here: 53.8 us
  Pallas kernels  53.2 us (99%)
  between operations  0.64 us (1%)
    pallas_call x1, Pallas kernels, local(): pl.pallas_call(functools.partial(kernel, n_row, n_col), out_shape=(pltpu....  51.6 us
    pallas_call x1, Pallas kernels, local(): pl.pallas_call(finish, out_shape=(jax.ShapeDtypeStruct(grad_wi.shape[1:],...  1.57 us

profile of v4, /device:TPU:1, one launch (start us, length us, event | category | flops | bytes accessed | tf_op | source)
XLA Modules:
  0.0 53.8 jit_solution(5944470819598069407)
XLA Ops:
  0.6 51.6 %adafactor.1 = (bf16[4,2,256,512]{3,2,1,0:T(8,128)(2,1)S(1)}, f32[10,128,128]{2,1,0:T(8,128)S(1)}, f32[16,128]{1,0:T(8,128)S(1)}, f32[4,128]{1,0:T(4,128)S(1)}, ...) custom-call(bf16[1,256,2048]{2,1,0:T(8,128)(2,1)} %grad_wi.1, ...), custom_call_target="tpu_custom_call" | custom-call | tf_op jit(solution)/shard_map/adafactor/pallas_call | solution.py:505
  52.2 1.6 %finish.1 = (bf16[256,2048]{1,0:T(8,128)(2,1)}, f32[2,128]{1,0:T(2,128)}, f32[16,128]{1,0:T(8,128)}, bf16[1024,512]{1,0:T(8,128)(2,1)}, f32[8,128]{1,0:T(8,128)}, /*index=5*/f32[4,128]{1,0:T(4,128)}) custom-call(bf16[4,2,256,512]{3,2,1,0:T(8,128)(2,1)S(1)} %get-tuple-element.20.total, f32[10,128,128]{2,1,0:T(8,128)S(1)} %get-tuple-element.21.row_scale, ...), custom_call_target="tpu_custom_call" | custom-call | tf_op jit(solution)/shard_map/finish/pallas_call | solution.py:551
